TPU v7x, 32 devices: a whole 2x2x4 slice. The times are simulated.
32 devices in a mesh: dom: 16 (over z, y, x), head: 2 (over core).
Axes of the slice: x: 2, y: 2, z: 4, core: 2. Of those that a mesh axis runs over, the one named last changes fastest.
Arguments:
- query_rows: bfloat16 [4096, 512], P('dom', 'head'), may hold values from -70 to 70
- key_rows: bfloat16 [4096, 512], P('dom', 'head'), may hold values from -4 to 4
- value_rows: bfloat16 [4096, 512], P('dom', 'head'), may hold values from -6 to 6
- out_weight: bfloat16 [512, 512], P('head'), may hold values from -0.25 to 0.25
- out_grad: bfloat16 [4096, 512], P('dom', 'head'), may hold values from -6 to 6
- far_bias: float32 [8], P('head'), may hold values from 4 to 7
- tile_list: int32 [32, 4], P('dom'), may hold values from 0 to 31, as said below
- tile_count: int32 [32], P('dom'), may hold values from 1 to 4, as said below
- send_rows: int32 [16, 16, 64], P('dom'), may hold values from 0 to 255
- expander_slot: int32 [4096, 3], P('dom'), may hold values from 0 to 1023, as said below
Outputs:
- layer_out: bfloat16 [4096, 512], P('dom', 'head')
- query_grad: bfloat16 [4096, 512], P('dom', 'head')
- key_grad: bfloat16 [4096, 512], P('dom', 'head')
- value_grad: bfloat16 [4096, 512], P('dom', 'head')
- out_weight_grad: float32 [512, 512], P('dom', 'head')
Inputs may be any that keep to these rules, and one draw needn't show every extreme that they name: `tile_list`: row t begins with t itself; its first tile_count[t] entries are distinct tiles from the 2 last tiles of the previous partition, the 2 tiles of t's own partition and the 2 first tiles of the next partition (partition = block of 2 tiles); later entries equal t. `tile_count`: every partition of 2 tiles has a tile with 4. `expander_slot`: A value names source partition value // 64 and slot value % 64 of send_rows[source, partition of the node].
All inputs are finite; a program needn't handle non-finite values.
Results may differ from a plain program's by a relative error of at most 0.011.
Values may be sent and summed in bfloat16 or wider, within the bound.
A program may use at most 64 MiB of HBM per device.

v0:
```python
import math

import jax
import jax.numpy as jnp
from jax import lax
from jax.sharding import PartitionSpec as P

TILE = 128
HALO = 2
DEG = 3


def extended_2(value, sides, width):
    for axis, dim in sides:
        peers, length = (lax.axis_size(axis), value.shape[dim])
        up = [(i, (i + 1) % peers) for i in range(peers - 1)]
        down = [(j, i) for i, j in up]
        last = lax.slice_in_dim(value, length - width, length, axis=dim)
        leading = lax.slice_in_dim(value, 0, width, axis=dim)
        before = lax.ppermute(last, axis, up)
        after = lax.ppermute(leading, axis, down)
        value = jnp.concatenate([before, value, after], axis=dim)
    return value


def from_behind(value, axis, steps):
    count = lax.axis_size(axis)
    leading, last = (max(0, -steps), min(count, count - steps))
    return lax.ppermute(value, axis, [(source, source + steps) for source in range(leading, last)])


def rounded(values):
    return lax.optimization_barrier(values.astype(jnp.bfloat16)).astype(jnp.float32)


def tile_work(query_tile, grad_tile, tile_ids, live_count, far_tile, ext_tiles, bias, base_tile):
    col_width = query_tile.shape[1]
    heads_here = bias.shape[0]
    head_size = col_width // heads_here
    score_scale = head_size ** (-0.5)
    key_block = ext_tiles[tile_ids - base_tile].reshape(-1, 2 * col_width)
    near_keys = key_block[:, :col_width].reshape(-1, heads_here, head_size)
    near_values = key_block[:, col_width:].reshape(-1, heads_here, head_size)
    far_keys = far_tile[:, :, :col_width].reshape(TILE, -1, heads_here, head_size)
    far_values = far_tile[:, :, col_width:].reshape(TILE, -1, heads_here, head_size)
    queries = query_tile.reshape(TILE, heads_here, head_size)
    upstream = grad_tile.reshape(TILE, heads_here, head_size)
    live_keys = jnp.repeat(jnp.arange(tile_ids.shape[0]) < live_count, TILE)
    near_score = (
        jnp.einsum("qhd,khd->hqk", queries, near_keys, preferred_element_type=jnp.float32)
        * score_scale
    )
    far_score = (
        jnp.einsum("qhd,qehd->hqe", queries, far_keys, preferred_element_type=jnp.float32)
        * score_scale
        + bias[:, None, None]
    )
    row_max = jnp.maximum(
        jnp.max(jnp.where(live_keys, near_score, -jnp.inf), axis=2), jnp.max(far_score, axis=2)
    )
    near_exp = jnp.where(live_keys, jnp.exp(near_score - row_max[:, :, None]), 0.0)
    far_exp = jnp.exp(far_score - row_max[:, :, None])
    row_sum = jnp.sum(near_exp, axis=2) + jnp.sum(far_exp, axis=2)
    mixed = jnp.einsum(
        "hqk,khd->qhd",
        near_exp.astype(jnp.bfloat16),
        near_values,
        preferred_element_type=jnp.float32,
    )
    mixed = mixed + jnp.einsum(
        "hqe,qehd->qhd",
        far_exp.astype(jnp.bfloat16),
        far_values,
        preferred_element_type=jnp.float32,
    )
    attention = (mixed / row_sum.T[:, :, None]).astype(jnp.bfloat16)
    delta_term = jnp.sum(
        upstream.astype(jnp.float32) * rounded(mixed / row_sum.T[:, :, None]), axis=2
    ).T
    near_dprob = jnp.einsum(
        "qhd,khd->hqk", upstream, near_values, preferred_element_type=jnp.float32
    )
    far_dprob = jnp.einsum(
        "qhd,qehd->hqe", upstream, far_values, preferred_element_type=jnp.float32
    )
    near_prob = near_exp / row_sum[:, :, None]
    far_prob = far_exp / row_sum[:, :, None]
    near_dscore = (near_prob * (near_dprob - delta_term[:, :, None])).astype(jnp.bfloat16)
    far_dscore = (far_prob * (far_dprob - delta_term[:, :, None])).astype(jnp.bfloat16)
    query_grad = jnp.einsum(
        "hqk,khd->qhd", near_dscore, near_keys, preferred_element_type=jnp.float32
    )
    query_grad = (
        query_grad
        + jnp.einsum("hqe,qehd->qhd", far_dscore, far_keys, preferred_element_type=jnp.float32)
    ) * score_scale
    near_kgrad = (
        jnp.einsum("hqk,qhd->khd", near_dscore, queries, preferred_element_type=jnp.float32)
        * score_scale
    )
    near_vgrad = jnp.einsum(
        "hqk,qhd->khd", near_prob.astype(jnp.bfloat16), upstream, preferred_element_type=jnp.float32
    )
    far_kgrad = (
        jnp.einsum("hqe,qhd->qehd", far_dscore, queries, preferred_element_type=jnp.float32)
        * score_scale
    )
    far_vgrad = jnp.einsum(
        "hqe,qhd->qehd", far_prob.astype(jnp.bfloat16), upstream, preferred_element_type=jnp.float32
    )
    near_grad = jnp.concatenate(
        [near_kgrad.reshape(-1, col_width), near_vgrad.reshape(-1, col_width)], axis=1
    )
    far_grad = jnp.concatenate(
        [far_kgrad.reshape(TILE, -1, col_width), far_vgrad.reshape(TILE, -1, col_width)], axis=2
    )
    return (
        attention.reshape(TILE, col_width),
        query_grad.astype(jnp.bfloat16).reshape(TILE, col_width),
        near_grad,
        far_grad,
    )


def shards(
    query_rows,
    key_rows,
    value_rows,
    out_weight,
    out_grad,
    far_bias,
    tile_list,
    tile_count,
    send_rows,
    expander_slot,
):
    col_width = query_rows.shape[1]
    node_count = query_rows.shape[0]
    per_part = node_count // TILE
    dom_index = lax.axis_index("dom")
    full_grad = lax.all_gather(out_grad, "head", axis=1, tiled=True)
    attn_grad = lax.dot_general(
        full_grad, out_weight, (((1,), (1,)), ((), ())), preferred_element_type=jnp.float32
    ).astype(jnp.bfloat16)
    stacked = jnp.concatenate([key_rows, value_rows], axis=1)
    rim_rows = HALO * TILE
    extended = extended_2(stacked, (("dom", 0),), rim_rows)
    ext_tiles = extended.reshape(-1, TILE, 2 * col_width)
    outgoing = stacked[send_rows[0]]
    received = lax.all_to_all(outgoing, "dom", split_axis=0, concat_axis=0, tiled=True)
    far_all = received.reshape(-1, 2 * col_width)[expander_slot]
    group = math.gcd(4, per_part)
    rounds = per_part // group
    base_tile = dom_index * per_part - HALO
    tile_lanes = jnp.arange(TILE, dtype=jnp.int32)
    batched = jax.vmap(tile_work, in_axes=(0, 0, 0, 0, 0, None, None, None))

    def advance(accum, inputs):
        query_group, grad_group, list_group, count_group, far_group = inputs
        attn_group, qgrad_group, near_group, fgrad_group = batched(
            query_group,
            grad_group,
            list_group,
            count_group,
            far_group,
            ext_tiles,
            far_bias,
            base_tile,
        )
        targets = ((list_group - base_tile)[:, :, None] * TILE + tile_lanes).reshape(-1)
        accum = accum.at[targets].add(near_group.reshape(-1, 2 * col_width))
        return (accum, (attn_group, qgrad_group, fgrad_group))

    inputs = (
        query_rows.reshape(rounds, group, TILE, col_width),
        attn_grad.reshape(rounds, group, TILE, col_width),
        tile_list.reshape(rounds, group, -1),
        tile_count.reshape(rounds, group),
        far_all.reshape(rounds, group, TILE, DEG, 2 * col_width),
    )
    start_grad = jnp.zeros((extended.shape[0], 2 * col_width), jnp.float32)
    ext_grad, (attn_all, qgrad_all, far_grad) = lax.scan(advance, start_grad, inputs)
    attn_mine = attn_all.reshape(node_count, col_width)
    low_part = ext_grad[:rim_rows]
    high_part = ext_grad[rim_rows + node_count :]
    own_grad = ext_grad[rim_rows : rim_rows + node_count]
    from_next = from_behind(low_part.astype(jnp.bfloat16), "dom", -1).astype(low_part.dtype)
    from_prev = from_behind(high_part.astype(jnp.bfloat16), "dom", 1).astype(high_part.dtype)
    own_grad = own_grad.at[:rim_rows].add(from_prev).at[node_count - rim_rows :].add(from_next)
    slot_grad = jnp.zeros((received.shape[0] * received.shape[1], 2 * col_width), jnp.float32)
    slot_grad = slot_grad.at[expander_slot.reshape(-1)].add(far_grad.reshape(-1, 2 * col_width))
    returned = lax.all_to_all(
        slot_grad.reshape(received.shape[0], received.shape[1], -1),
        "dom",
        split_axis=0,
        concat_axis=0,
        tiled=True,
    )
    own_grad = own_grad.at[send_rows[0].reshape(-1)].add(returned.reshape(-1, 2 * col_width))
    key_grad = own_grad[:, :col_width].astype(jnp.bfloat16)
    value_grad = own_grad[:, col_width:].astype(jnp.bfloat16)
    attn_full = lax.all_gather(attn_mine, "head", axis=1, tiled=True)
    weight_block = lax.all_to_all(out_weight, "head", split_axis=1, concat_axis=0, tiled=True)
    layer_out = jnp.dot(attn_full, weight_block, preferred_element_type=jnp.float32).astype(
        jnp.bfloat16
    )
    out_weight_grad = lax.psum_scatter(
        lax.dot_general(
            full_grad, attn_mine, (((0,), (0,)), ((), ())), preferred_element_type=jnp.float32
        ),
        "dom",
        scatter_dimension=0,
        tiled=True,
    )
    return (
        layer_out,
        qgrad_all.reshape(node_count, col_width),
        key_grad,
        value_grad,
        out_weight_grad,
    )


def solution(mesh):
    in_specs = (
        P("dom", "head"),
        P("dom", "head"),
        P("dom", "head"),
        P("head", None),
        P("dom", "head"),
        P("head"),
        P("dom", None),
        P("dom"),
        P("dom", None, None),
        P("dom", None),
    )
    out_specs = (
        P("dom", "head"),
        P("dom", "head"),
        P("dom", "head"),
        P("dom", "head"),
        P("dom", "head"),
    )
    return jax.shard_map(shards, mesh=mesh, in_specs=in_specs, out_specs=out_specs, check_vma=False)
```

profile of v0, /device:TPU:0, one launch (start us, length us, event | category | flops | bytes accessed | tf_op | source)
XLA Modules:
  0.0 229.7 jit_solution(2960010280147900423)
XLA Ops:
  10.3 5.5 %collective-permute-start = (bf16[256,512]{1,0:T(8,128)(2,1)S(1)}, bf16[256,512]{1,0:T(8,128)(2,1)S(1)}, u32[]{:S(2)}, u32[]{:S(2)}) collective-permute-start(bf16[256,512]{1,0:T(8,128)(2,1)S(1)} %constant_dynamic-update-slice_fusion), channel_id=1, source_target_pairs={{0,2},{2,4},{4,6},{6,8},{8,10},{10,12},{12,14},{14,16},{16,18},{18... | collective-permute-start | bytes 786440 | tf_op jit(solution)/shard_map/ppermute | solution.py:20
  16.6 5.1 %gather_fusion.1 = bf16[1024,512]{1,0:T(8,128)(2,1)} fusion(bf16[256,512]{1,0:T(8,128)(2,1)S(1)} %constant_dynamic-update-slice_fusion, s32[1024]{0:T(1024)S(1)} %broadcast_clamp_fusion), kind=kCustom, calls=%fused_computation.1 | custom fusion | bytes 2101248 | tf_op jit(solution)/shard_map/gather | solution.py:149
  21.7 8.3 %all-to-all-start = ((bf16[16,64,512]{2,1,0:T(8,128)(2,1)}), bf16[16,64,512]{2,1,0:T(8,128)(2,1)S(1)}, u32[]{:S(2)}, u32[]{:S(2)}) async-start(bf16[16,64,512]{2,1,0:T(8,128)(2,1)} %bitcast.13), calls=%async_computation | async-start | bytes 2097152 | tf_op jit(solution)/shard_map/all_to_all | solution.py:150
  30.1 2.0 all_gather.7
  42.1 1.7 select_reduce_fusion
  43.9 10.0 %all-to-all-done = bf16[16,64,512]{2,1,0:T(8,128)(2,1)S(1)} async-done(((bf16[16,64,512]{2,1,0:T(8,128)(2,1)}), bf16[16,64,512]{2,1,0:T(8,128)(2,1)S(1)}, u32[]{:S(2)}, u32[]{:S(2)}) %all-to-all-start) | async-done | bytes 1048608 | tf_op jit(solution)/shard_map/all_to_all | solution.py:150
  53.9 4.3 %all-to-all-start.1 = ((bf16[256,2,256]{0,2,1:T(8,128)(2,1)}), bf16[256,2,256]{0,2,1:T(8,128)(2,1)}, u32[]{:S(2)}, u32[]{:S(2)}) async-start(bf16[256,2,256]{0,2,1:T(8,128)(2,1)} %bitcast.24), calls=%async_computation.1 | async-start | bytes 524288 | tf_op jit(solution)/shard_map/all_to_all | solution.py:203
  58.2 3.3 %gather_fusion.2 = bf16[768,512]{1,0:T(8,128)(2,1)} fusion(bf16[1024,512]{1,0:T(8,128)(2,1)S(1)} %bitcast.123, s32[1024]{0:T(1024)S(1)} %pad_clamp_fusion), kind=kCustom, calls=%fused_computation.2 | custom fusion | bytes 1575936 | tf_op jit(solution)/shard_map/gather | solution.py:151
  61.5 2.4 %squeeze.20 = bf16[2,128,3,512]{3,2,1,0:T(4,128)(2,1)S(1)} reshape(bf16[768,512]{1,0:T(8,128)(2,1)} %gather_fusion.2) | data formatting | bytes 1572864 | tf_op jit(solution)/shard_map/while/body/jit(dynamic_index_in_dim)/squeeze | solution.py:182
  69.9 1.8 fusion.31
  72.9 1.7 bitcast_reduce_fusion
  76.2 1.7 multiply_reduce_fusion.1
  77.8 1.7 copy.181
  81.2 1.7 fusion.9
  84.3 2.5 %convert_bitcast_fusion.1 = (f32[2,128,4,3]{2,3,1,0:T(4,128)}, bf16[2,4,128,3]{1,3,2,0:T(4,128)(2,1)}, f32[2,128,4,3]{2,3,1,0:T(4,128)S(1)}) fusion(f32[2,4,128,3]{1,3,2,0:T(4,128)} %copy.181, f32[2,4,128]{1,2,0:T(8,128)} %copy.142, f32[2,4,128]{1,2,0:T(8,128)} %copy.141, f32[2,4,128]{1,2,0:T(8,128)} %copy-done.10, f32[4]{0:T(128)S(1)} %copy-done.32, ...), kind=kLoop, calls=%fused_computation.49 | loop fusion | flops 30720 | bytes 67600 | tf_op jit(solution)/shard_map/convert.6
  86.8 1.9 multiply_bitcast_fusion
  88.7 2.2 concatenate.36
  90.9 2.9 %multiply_bitcast_fusion.1 = f32[2,128,3,4,64]{4,3,2,1,0:T(4,128)} fusion(f32[2,128,4,64]{3,2,1,0:T(4,128)} %copy.152, f32[2,128,4,3]{2,3,1,0:T(4,128)} %get-tuple-element.112), kind=kLoop, calls=%fused_computation.18 | loop fusion | flops 393216 | bytes 1060864 | tf_op jit(solution)/shard_map/while/body/eval_jaxpr/vmap()/mul | solution.py:105
  93.9 3.0 %concatenate.35 = f32[768,256]{1,0:T(8,128)} reshape(f32[2,128,3,4,64]{4,3,2,1,0:T(4,128)} %multiply_bitcast_fusion.1) | data formatting | bytes 1572864 | tf_op jit(solution)/shard_map/while/body/eval_jaxpr/vmap()/concatenate | solution.py:114
  96.9 8.7 %scatter_custom_fusion.1 = f32[1024,512]{1,0:T(8,128)} fusion(s32[768]{0:T(1024)} %fusion.26, f32[768,256]{1,0:T(8,128)S(1)} %concatenate.36, f32[]{:T(128)} %constant.132.clone.1, f32[768,256]{1,0:T(8,128)} %concatenate.35, f32[]{:T(128)} %constant.135.clone.1), kind=kCustom, calls=%fused_computation.13 | custom fusion | flops 786432 | bytes 3671040 | tf_op jit(solution)/shard_map/scatter-add | solution.py:191
  105.6 6.0 %all-to-all-start.2 = ((f32[16,64,512]{2,1,0:T(8,128)}), f32[16,64,512]{2,1,0:T(8,128)}, u32[]{:S(2)}, u32[]{:S(2)}) async-start(f32[16,64,512]{2,1,0:T(8,128)} %bitcast.124), calls=%async_computation.2 | async-start | bytes 4194304 | tf_op jit(solution)/shard_map/all_to_all | solution.py:192
  111.8 1.8 copy.135
  115.9 1.7 convolution_bitcast_fusion
  121.5 1.8 copy.150
  123.3 7.6 %scatter_custom_fusion = f32[768,512]{1,0:T(8,128)S(1)} fusion(s32[1024]{0:T(1024)} %bitcast.151, f32[1024,512]{1,0:T(8,128)} %copy.150, f32[]{:T(128)} %constant.135.clone.1), kind=kCustom, calls=%fused_computation.44 | custom fusion | flops 524288 | bytes 1573376 | tf_op jit(solution)/shard_map/while/body/eval_jaxpr/scatter-add | solution.py:171
  133.2 5.3 %collective-permute-start.2 = (bf16[256,512]{1,0:T(8,128)(2,1)}, bf16[256,512]{1,0:T(8,128)(2,1)}, u32[]{:S(2)}, u32[]{:S(2)}) collective-permute-start(bf16[256,512]{1,0:T(8,128)(2,1)} %get-tuple-element.119), channel_id=1, source_target_pairs={{0,2},{2,4},{4,6},{6,8},{8,10},{10,12},{12,14},{14,16},{16,18},{18... | collective-permute-start | bytes 786440 | tf_op jit(solution)/shard_map/ppermute | solution.py:29
  139.5 2.0 copy.196
  142.5 2.0 all_gather.6
  146.5 2.6 %collective-permute-done.3 = bf16[256,512]{1,0:T(8,128)(2,1)} collective-permute-done((bf16[256,512]{1,0:T(8,128)(2,1)}, bf16[256,512]{1,0:T(8,128)(2,1)}, u32[]{:S(2)}, u32[]{:S(2)}) %collective-permute-start.3) | collective-permute-done | bytes 262176 | tf_op jit(solution)/shard_map/ppermute | solution.py:29
  149.1 11.2 %collective-permute-done.2 = bf16[256,512]{1,0:T(8,128)(2,1)} collective-permute-done((bf16[256,512]{1,0:T(8,128)(2,1)}, bf16[256,512]{1,0:T(8,128)(2,1)}, u32[]{:S(2)}, u32[]{:S(2)}) %collective-permute-start.2) | collective-permute-done | bytes 262176 | tf_op jit(solution)/shard_map/ppermute | solution.py:29
  161.4 7.5 %scatter_fusion = f32[256,512]{1,0:T(8,128)S(1)} fusion(f32[256,512]{1,0:T(8,128)S(1)} %fusion.19, s32[1024]{0:T(1024)S(1)} %bitcast.148, f32[1024,512]{1,0:T(8,128)} %bitcast.43), kind=kCustom, calls=%fused_computation.5 | custom fusion | flops 524288 | bytes 6295552 | tf_op jit(solution)/shard_map/scatter-add | solution.py:199
  169.7 53.1 %reduce-scatter.4.cloned.1.call-done = f32[32,256]{1,0:T(8,128)} async-done(((f32[512,256]{1,0:T(8,128)}), f32[32,256]{1,0:T(8,128)}) %reduce-scatter.4.cloned.1.call-update) | async-done | bytes 32784
  (158 shorter events, 39.9 us)
Async XLA Ops:
  9.0 30.4 %collective-permute-start.1 = (bf16[256,512]{1,0:T(8,128)(2,1)S(1)}, bf16[256,512]{1,0:T(8,128)(2,1)S(1)}, u32[]{:S(2)}, u32[]{:S(2)}) collective-permute-start(bf16[256,512]{1,0:T(8,128)(2,1)S(1)} %constant_dynamic-update-slice_fusion), channel_id=1, source_target_pairs={{2,0},{4,2},{6,4},{8,6},{10,8},{12,10},{14,12},{16,14},{18,16},{20... | collective-permute-start | bytes 786440 | tf_op jit(solution)/shard_map/ppermute | solution.py:21
  10.3 29.1 %collective-permute-start = (bf16[256,512]{1,0:T(8,128)(2,1)S(1)}, bf16[256,512]{1,0:T(8,128)(2,1)S(1)}, u32[]{:S(2)}, u32[]{:S(2)}) collective-permute-start(bf16[256,512]{1,0:T(8,128)(2,1)S(1)} %constant_dynamic-update-slice_fusion), channel_id=1, source_target_pairs={{0,2},{2,4},{4,6},{6,8},{8,10},{10,12},{12,14},{14,16},{16,18},{18... | collective-permute-start | bytes 786440 | tf_op jit(solution)/shard_map/ppermute | solution.py:20
  21.7 8.4 %copy-start.30 = (s32[256,3]{0,1:T(4,128)S(1)}, s32[256,3]{0,1:T(4,128)}, u32[]{:S(2)}) copy-start(s32[256,3]{0,1:T(4,128)} %param.27) | copy-start | bytes 9220
  21.7 8.4 %copy-start.35 = (s32[2]{0:T(128)S(1)}, s32[2]{0:T(128)}, u32[]{:S(2)}) copy-start(s32[2]{0:T(128)} %param.25) | copy-start | bytes 28
  21.7 8.5 %copy-start.20 = (bf16[256,256]{1,0:T(8,128)(2,1)S(1)}, bf16[256,256]{1,0:T(8,128)(2,1)}, u32[]{:S(2)}) copy-start(bf16[256,256]{1,0:T(8,128)(2,1)} %param.22) | copy-start | bytes 393220
  21.7 10.4 %copy-start.14 = (bf16[256,512]{1,0:T(8,128)(2,1)S(1)}, bf16[256,512]{1,0:T(8,128)(2,1)}, u32[]{:S(2)}) copy-start(bf16[256,512]{1,0:T(8,128)(2,1)} %param.21) | copy-start | bytes 786436
  21.7 11.1 %copy-start.21 = (bf16[256,256]{1,0:T(8,128)(2,1)S(1)}, bf16[256,256]{1,0:T(8,128)(2,1)}, u32[]{:S(2)}) copy-start(bf16[256,256]{1,0:T(8,128)(2,1)} %param.18) | copy-start | bytes 393220
  21.7 11.5 %copy-start.34 = (s32[2,4]{1,0:T(2,128)S(1)}, s32[2,4]{1,0:T(2,128)}, u32[]{:S(2)}) copy-start(s32[2,4]{1,0:T(2,128)} %param.24) | copy-start | bytes 100
  21.7 32.2 %all-to-all-start = ((bf16[16,64,512]{2,1,0:T(8,128)(2,1)}), bf16[16,64,512]{2,1,0:T(8,128)(2,1)S(1)}, u32[]{:S(2)}, u32[]{:S(2)}) async-start(bf16[16,64,512]{2,1,0:T(8,128)(2,1)} %bitcast.13), calls=%async_computation | async-start | bytes 2097152 | tf_op jit(solution)/shard_map/all_to_all | solution.py:150
  32.1 3.9 %copy-start.3 = (bf16[256,512]{1,0:T(8,128)(2,1)}, bf16[256,512]{1,0:T(8,128)(2,1)S(1)}, u32[]{:S(2)}) copy-start(bf16[256,512]{1,0:T(8,128)(2,1)S(1)} %all_gather.7) | copy-start | bytes 786436
  33.0 9.2 %copy-start.1 = (bf16[2,128,4,64]{1,0,3,2:T(2,128)(2,1)}, bf16[2,128,4,64]{1,0,3,2:T(2,128)(2,1)S(1)}, u32[]{:S(2)}) copy-start(bf16[2,128,4,64]{1,0,3,2:T(2,128)(2,1)S(1)} %reshape.302) | copy-start | bytes 393220
  33.1 5.6 %copy-start.6 = (bf16[2,128,4,64]{1,0,3,2:T(2,128)(2,1)}, bf16[2,128,4,64]{1,0,3,2:T(2,128)(2,1)S(1)}, u32[]{:S(2)}) copy-start(bf16[2,128,4,64]{1,0,3,2:T(2,128)(2,1)S(1)} %reshape.307) | copy-start | bytes 393220
  36.0 6.2 %copy-start.23 = (pred[1,2,4,128]{3,1,2,0:T(4,128)(4,1)}, pred[1,2,4,128]{3,1,2,0:T(4,128)(4,1)S(1)}, u32[]{:S(2)}) copy-start(pred[1,2,4,128]{3,1,2,0:T(4,128)(4,1)S(1)} %copy.228) | copy-start | bytes 3076
  53.9 51.7 %all-to-all-start.1 = ((bf16[256,2,256]{0,2,1:T(8,128)(2,1)}), bf16[256,2,256]{0,2,1:T(8,128)(2,1)}, u32[]{:S(2)}, u32[]{:S(2)}) async-start(bf16[256,2,256]{0,2,1:T(8,128)(2,1)} %bitcast.24), calls=%async_computation.1 | async-start | bytes 524288 | tf_op jit(solution)/shard_map/all_to_all | solution.py:203
  63.9 5.3 %copy-start.31 = (f32[4]{0:T(128)S(1)}, f32[4]{0:T(128)}, u32[]{:S(2)}) copy-start(f32[4]{0:T(128)} %param.23) | copy-start | bytes 52
  69.9 7.9 %copy-start.10 = (f32[2,4,128]{1,2,0:T(8,128)}, f32[2,4,128]{1,2,0:T(8,128)S(1)}, u32[]{:S(2)}) copy-start(f32[2,4,128]{1,2,0:T(8,128)S(1)} %copy.130) | copy-start | bytes 12292
  82.9 3.9 %copy-start.5 = (f32[2,128,4,64]{3,2,1,0:T(4,128)S(1)}, f32[2,128,4,64]{3,2,1,0:T(4,128)}, u32[]{:S(2)}) copy-start(f32[2,128,4,64]{3,2,1,0:T(4,128)} %copy.153) | copy-start | bytes 786436
  83.5 5.2 %copy-start.25 = (f32[2,128,4]{1,2,0:T(4,128)}, f32[2,128,4]{1,2,0:T(4,128)S(1)}, u32[]{:S(2)}) copy-start(f32[2,128,4]{1,2,0:T(4,128)S(1)} %multiply_reduce_fusion.4) | copy-start | bytes 12292
  105.5 6.1 %copy-start.22 = (s32[1,16,64]{2,1,0:T(8,128)S(1)}, s32[1,16,64]{2,1,0:T(8,128)}, u32[]{:S(2)}) copy-start(s32[1,16,64]{2,1,0:T(8,128)} %param.26) | copy-start | bytes 12292
  105.5 8.0 %copy-start.33 = (s32[2,4]{1,0:T(2,128)S(1)}, s32[2,4]{1,0:T(2,128)}, u32[]{:S(2)}) copy-start(s32[2,4]{1,0:T(2,128)} %get-tuple-element.125) | copy-start | bytes 100
  105.5 9.3 %copy-start.19 = (bf16[2,128,4,64]{1,3,2,0:T(8,128)(2,1)S(1)}, bf16[2,128,4,64]{1,3,2,0:T(8,128)(2,1)}, u32[]{:S(2)}) copy-start(bf16[2,128,4,64]{1,3,2,0:T(8,128)(2,1)} %copy-done.18) | copy-start | bytes 393220
  105.6 10.1 %copy-start.13 = (bf16[2,4,128,3]{1,3,2,0:T(4,128)(2,1)S(1)}, bf16[2,4,128,3]{1,3,2,0:T(4,128)(2,1)}, u32[]{:S(2)}) copy-start(bf16[2,4,128,3]{1,3,2,0:T(4,128)(2,1)} %get-tuple-element.113) | copy-start | bytes 18436
  105.6 55.9 %all-to-all-start.2 = ((f32[16,64,512]{2,1,0:T(8,128)}), f32[16,64,512]{2,1,0:T(8,128)}, u32[]{:S(2)}, u32[]{:S(2)}) async-start(f32[16,64,512]{2,1,0:T(8,128)} %bitcast.124), calls=%async_computation.2 | async-start | bytes 4194304 | tf_op jit(solution)/shard_map/all_to_all | solution.py:192
  111.6 4.2 %copy-start.8 = (bf16[2,128,4,64]{1,0,3,2:T(2,128)(2,1)S(1)}, bf16[2,128,4,64]{1,0,3,2:T(2,128)(2,1)}, u32[]{:S(2)}) copy-start(bf16[2,128,4,64]{1,0,3,2:T(2,128)(2,1)} %copy-done.6) | copy-start | bytes 393220
  111.6 111.2 %reduce-scatter.4.cloned.1.call-start = ((), (), s32[]{:S(2)}) async-start(), calls=%async_computation.4 | async-start | bytes 557056
  131.0 7.5 %copy-start.4 = (bf16[256,512]{1,0:T(8,128)(2,1)S(1)}, bf16[256,512]{1,0:T(8,128)(2,1)}, u32[]{:S(2)}) copy-start(bf16[256,512]{1,0:T(8,128)(2,1)} %copy-done.3) | copy-start | bytes 786436
  131.0 7.5 %copy-start.12 = (bf16[2,128,4,64]{1,0,3,2:T(2,128)(2,1)S(1)}, bf16[2,128,4,64]{1,0,3,2:T(2,128)(2,1)}, u32[]{:S(2)}) copy-start(bf16[2,128,4,64]{1,0,3,2:T(2,128)(2,1)} %copy-done.11) | copy-start | bytes 393220
  131.1 10.6 %copy-start = (bf16[2,512,256]{1,2,0:T(8,128)(2,1)S(1)}, bf16[2,512,256]{1,2,0:T(8,128)(2,1)}, u32[]{:S(2)}) copy-start(bf16[2,512,256]{1,2,0:T(8,128)(2,1)} %copy.123) | copy-start | bytes 1572868
  132.0 17.1 %collective-permute-start.3 = (bf16[256,512]{1,0:T(8,128)(2,1)}, bf16[256,512]{1,0:T(8,128)(2,1)}, u32[]{:S(2)}, u32[]{:S(2)}) collective-permute-start(bf16[256,512]{1,0:T(8,128)(2,1)} %get-tuple-element.120), channel_id=1, source_target_pairs={{2,0},{4,2},{6,4},{8,6},{10,8},{12,10},{14,12},{16,14},{18,16},{20... | collective-permute-start | bytes 786440 | tf_op jit(solution)/shard_map/ppermute | solution.py:29
  133.2 27.1 %collective-permute-start.2 = (bf16[256,512]{1,0:T(8,128)(2,1)}, bf16[256,512]{1,0:T(8,128)(2,1)}, u32[]{:S(2)}, u32[]{:S(2)}) collective-permute-start(bf16[256,512]{1,0:T(8,128)(2,1)} %get-tuple-element.119), channel_id=1, source_target_pairs={{0,2},{2,4},{4,6},{6,8},{8,10},{10,12},{12,14},{14,16},{16,18},{18... | collective-permute-start | bytes 786440 | tf_op jit(solution)/shard_map/ppermute | solution.py:29
  141.7 3.9 %copy-start.15 = (bf16[2,256,256]{2,1,0:T(8,128)(2,1)S(1)}, bf16[2,256,256]{2,1,0:T(8,128)(2,1)}, u32[]{:S(2)}) copy-start(bf16[2,256,256]{2,1,0:T(8,128)(2,1)} %copy.135) | copy-start | bytes 786436
  142.1 19.4 %copy-start.27 = (s32[1024,1]{0,1:T(1,128)S(1)}, s32[1024,1]{0,1:T(1,128)}, u32[]{:S(2)}) copy-start(s32[1024,1]{0,1:T(1,128)} %compare_select_fusion) | copy-start | bytes 12292
  (12 other events, 14.5 us)
Sparse Core Ops, SparseCore 0:
  141.7 81.0 reduce-scatter.3
where the time goes:
time: 231 us; the launch traced here: 230 us
  waiting for transfers between devices  76.9 us (33%)
  local copies, waits for them, and re-layouts  49.2 us (21%)
  other arithmetic  43.6 us (19%)
  starting transfers between devices  32 us (14%)
  between operations  14.7 us (6%)
  matrix products  9.14 us (4%)
  blocking collectives  3.96 us (2%)
    unnamed x2, waiting for transfers between devices  53.2 us
    ppermute x2, waiting for transfers between devices, from_behind(): lax.ppermute(value, axis, [(source, source + steps) for source in range(l...  13.8 us
    unnamed x90, local copies, waits for them, and re-layouts  12.9 us
    all_to_all x1, waiting for transfers between devices, shards(): lax.all_to_all(outgoing, 'dom', split_axis=0, concat_axis=0, tiled=True)  9.99 us
    scatter-add x1, other arithmetic, shards(): slot_grad.at[expander_slot.reshape(-1)]  8.69 us
    all_to_all x1, starting transfers between devices, shards(): lax.all_to_all(outgoing, 'dom', split_axis=0, concat_axis=0, tiled=True)  8.31 us
    scatter-add x1, other arithmetic, advance(): accum = accum.at[targets].add(near_group.reshape(-1, 2 * col_width))  7.63 us
    scatter-add x1, other arithmetic, shards(): own_grad.at[send_rows[0].reshape(-1)]  7.48 us
  transfers between devices with their start and end apart: 8, of which 4 were waited for; matrix products, arithmetic and copies ran while one was open for 43% of the time, Pallas kernels for 0%

commit v1 on v0

v1 whole, which is shorter than its diff:
```python
import functools

import jax
import jax.numpy as jnp
from jax import lax
from jax.experimental import pallas as pl
from jax.experimental.pallas import tpu as pltpu
from jax.sharding import PartitionSpec as P

TILE = 128
MESH = pl.DeviceIdType.MESH
F32 = jnp.float32
BF16 = jnp.bfloat16


def dot(a, b):
    return jnp.dot(a, b, preferred_element_type=F32)


def dot_nt(a, b):
    return lax.dot_general(a, b, (((1,), (1,)), ((), ())), preferred_element_type=F32)


def dot_tn(a, b):
    return lax.dot_general(a, b, (((0,), (0,)), ((), ())), preferred_element_type=F32)


def split_dot(x, m):
    hi = x.astype(BF16)
    lo = (x - hi.astype(F32)).astype(BF16)
    return dot(hi, m) + dot(lo, m)


def iota(shape, dim):
    return lax.broadcasted_iota(jnp.int32, shape, dim)


def slabs(flat, count, rows):
    return flat.reshape(count, rows, flat.shape[1])


def flat_of(stack):
    count, rows, width = stack.shape
    if rows % 16:
        return stack.astype(F32).reshape(count * rows, width).astype(BF16)
    return stack.reshape(count * rows, width)


def body(
    n, q_ref, k_ref, v_ref, w_ref, g_ref, bias_ref, list_ref, count_ref, rows_ref, slot_ref,
    lo_ref, qg_ref, kg_ref, vg_ref, dw_ref,
    kx, vx, out_far, in_far, back_out, back_in, g_oth, w_oth, att_mine, att_oth,
    rim_out, rim_in, dw_out, dw_in, exps, dprobs, mask_s, near_mix, near_max, near_sum,
    kgrad, vgrad, qgrad, far_t, rows_t, da_s, wide,
    far_ss, far_rs, rim_ss, rim_rs, bck_ss, bck_rs, rbk_ss, rbk_rs, dw_ss, dw_rs, hd_ss, hd_rs,
):
    me = lax.axis_index("dom")
    hd = lax.axis_index("head")
    nodes, cw = q_ref.shape
    heads = bias_ref.shape[0]
    hsize = cw // heads
    scale = hsize ** (-0.5)
    cap = out_far.shape[1]
    slots = n * cap
    deg = slot_ref.shape[1]
    tpd = nodes // TILE
    drows = dw_ref.shape[0]
    prev, nxt = lax.rem(me + n - 1, n), lax.rem(me + 1, n)

    barrier = pltpu.get_barrier_semaphore()

    def greet(i, _):
        pl.semaphore_signal(barrier, inc=1, device_id={"dom": lax.rem(me + i, n)}, device_id_type=MESH)
        return _

    lax.fori_loop(1, n, greet, 0)
    pl.semaphore_signal(barrier, inc=1, device_id={"head": 1 - hd}, device_id_type=MESH)
    pl.semaphore_wait(barrier, n)

    def to_dom(src, dst, ss, rs, d):
        return pltpu.make_async_remote_copy(
            src_ref=src, dst_ref=dst, send_sem=ss, recv_sem=rs, device_id={"dom": d}, device_id_type=MESH
        )

    def to_head(src, dst, i):
        return pltpu.make_async_remote_copy(
            src_ref=src, dst_ref=dst, send_sem=hd_ss.at[i], recv_sem=hd_rs.at[i],
            device_id={"head": 1 - hd}, device_id_type=MESH,
        )

    my_cols = pl.ds(pl.multiple_of(hd * cw, cw), cw)
    oth_cols = pl.ds(pl.multiple_of((1 - hd) * cw, cw), cw)
    send_g = to_head(g_ref, g_oth, 0)
    send_w = to_head(w_ref.at[:, oth_cols], w_oth, 1)
    send_att = to_head(att_mine, att_oth, 2)

    def rim_copies(low):
        d, at = (prev, 2) if low else (nxt, 0)
        s = 0 if low else 2
        return (
            to_dom(k_ref, kx.at[at], rim_ss.at[s], rim_rs.at[s], d),
            to_dom(v_ref, vx.at[at], rim_ss.at[s + 1], rim_rs.at[s + 1], d),
        )

    def rim_back(low):
        d, s = (prev, 0) if low else (nxt, 1)
        return to_dom(rim_out.at[s], rim_in.at[1 - s], rbk_ss.at[s], rbk_rs.at[s], d)

    def far_copy(d, s):
        return to_dom(out_far.at[d], in_far.at[s], far_ss.at[d], far_rs.at[s], d)

    def back_copy(d, s):
        return to_dom(back_out.at[d], back_in.at[s], bck_ss.at[d], bck_rs.at[s], d)

    def dw_copy(d, s):
        return to_dom(dw_out.at[d], dw_in.at[s], dw_ss.at[d], dw_rs.at[s], d)

    def every(fn):
        def step(i, _):
            fn(lax.rem(me + i, n))
            return _

        lax.fori_loop(1, n, step, 0)

    kv = jnp.concatenate([k_ref[...], v_ref[...]], axis=1)
    row_col = jnp.transpose(jnp.broadcast_to(rows_ref[...], (128, slots)))[:, 0:1]
    pick = (row_col == iota((slots, nodes), 1)).astype(F32).astype(BF16)
    picked = dot(pick, kv)
    if cap % 16:
        out_far[...] = slabs(picked, n, cap).astype(BF16)
    else:
        out_far[...] = slabs(picked.astype(BF16), n, cap)
    every(lambda d: far_copy(d, me).start())
    send_g.start()

    @pl.when(me > 0)
    def _():
        for c in rim_copies(True):
            c.start()

    @pl.when(me < n - 1)
    def _():
        for c in rim_copies(False):
            c.start()

    send_w.start()
    in_far[pl.ds(me, 1)] = out_far[pl.ds(me, 1)]

    kx[1] = k_ref[...]
    vx[1] = v_ref[...]

    @pl.when(me == 0)
    def _():
        kx[0] = jnp.zeros((nodes, cw), BF16)
        vx[0] = jnp.zeros((nodes, cw), BF16)
        rim_in[0] = jnp.zeros(rim_in.shape[1:], BF16)

    @pl.when(me == n - 1)
    def _():
        kx[2] = jnp.zeros((nodes, cw), BF16)
        vx[2] = jnp.zeros((nodes, cw), BF16)
        rim_in[1] = jnp.zeros(rim_in.shape[1:], BF16)

    rows_t[...] = (rows_ref[...] == iota((nodes, slots), 0)).astype(F32).astype(BF16)
    for e in range(deg):
        col = slot_ref[:, e : e + 1]
        row = jnp.transpose(jnp.broadcast_to(col, (nodes, 128)))[0:1, :]
        far_t[:, e * nodes : (e + 1) * nodes] = (row == iota((slots, nodes), 0)).astype(F32).astype(BF16)
    for t in range(tpd):
        for c in range(3 * tpd):
            live = jnp.int32(0)
            for j in range(list_ref.shape[1]):
                hit = (list_ref[t, j] == me * tpd + (c - tpd)) & (j < count_ref[t])
                live = jnp.maximum(live, hit.astype(jnp.int32))
            off = (1 - live).astype(F32) * jnp.float32(-1e30)
            mask_s[t * TILE : (t + 1) * TILE, c * TILE : (c + 1) * TILE] = jnp.full((TILE, TILE), off, F32)

    send_g.wait_recv()
    da_s[...] = (dot_nt(g_ref[...], w_ref[:, my_cols]) + dot_nt(g_oth[...], w_ref[:, oth_cols])).astype(BF16)
    lane = iota((nodes, 128), 1)
    col_head = iota((nodes, cw), 1) // hsize
    near_mix[...] = jnp.zeros((nodes, cw), F32)
    near_max[...] = jnp.zeros((nodes, 128), F32)
    near_sum[...] = jnp.ones((nodes, 128), F32)

    @pl.when(me > 0)
    def _():
        for c in rim_copies(False):
            c.wait_recv()

    @pl.when(me < n - 1)
    def _():
        for c in rim_copies(True):
            c.wait_recv()

    ext = 3 * nodes

    def near_head(h, _):
        here = col_head == h
        keys = kx[...].reshape(ext, cw)
        values = vx[...].reshape(ext, cw)
        qh = jnp.where(here, q_ref[...], jnp.zeros((), BF16))
        dah = jnp.where(here, da_s[...], jnp.zeros((), BF16))
        score = dot_nt(qh, keys) * scale + mask_s[...]
        top = jnp.max(score, axis=1, keepdims=True)
        ex = jnp.exp(score - top)
        exps[h] = ex
        near_max[...] = jnp.where(lane == h, top, near_max[...])
        near_sum[...] = jnp.where(lane == h, jnp.sum(ex, axis=1, keepdims=True), near_sum[...])
        near_mix[...] = jnp.where(here, dot(ex.astype(BF16), values), near_mix[...])
        dprobs[h] = dot_nt(dah, values)
        return _

    lax.fori_loop(0, heads, near_head, 0)

    every(lambda s: far_copy(s, s).wait_recv())
    fold = (iota((cw, 128), 0) // hsize == iota((cw, 128), 1)).astype(F32).astype(BF16)
    spread = (iota((128, cw), 0) == iota((128, cw), 1) // hsize).astype(F32).astype(BF16)
    bias = jnp.zeros((1, 128), F32)
    for h in range(heads):
        bias = jnp.where(iota((1, 128), 1) == h, bias_ref[h], bias)
    received = flat_of(in_far[...])
    q32 = q_ref[...].astype(F32)
    da32 = da_s[...].astype(F32)
    far_s = []
    for e in range(deg):
        hot = (slot_ref[:, e : e + 1] == iota((nodes, slots), 1)).astype(F32).astype(BF16)
        wide[e] = dot(hot, received)
        far_s.append(split_dot(q32 * wide[e, :, :cw], fold) * scale + bias)
    top_n = near_max[...]
    top = top_n
    for s in far_s:
        top = jnp.maximum(top, s)
    near_f = jnp.exp(top_n - top)
    far_x = [jnp.exp(s - top) for s in far_s]
    total = near_sum[...] * near_f
    for x in far_x:
        total = total + x
    inv = 1.0 / total
    mixed = near_mix[...] * split_dot(near_f, spread)
    for e in range(deg):
        mixed = mixed + dot(far_x[e].astype(BF16), spread) * wide[e, :, cw:]
    att = (mixed * split_dot(inv, spread)).astype(BF16)
    att_mine[...] = att
    send_att.start()
    delta = split_dot(da32 * att.astype(F32), fold)
    qg = jnp.zeros((nodes, cw), F32)
    parts = []
    for e in range(deg):
        prob = far_x[e] * inv
        dp = split_dot(da32 * wide[e, :, cw:], fold)
        ds = dot((prob * (dp - delta)).astype(BF16), spread)
        qg = qg + ds * wide[e, :, :cw]
        parts.append(
            jnp.concatenate(
                [(ds * q32 * scale).astype(BF16), (dot(prob.astype(BF16), spread) * da32).astype(BF16)], axis=1
            )
        )
    qgrad[...] = qg
    slot_grad = dot(far_t[...], jnp.concatenate(parts, axis=0))
    if cap % 16:
        back_out[...] = slabs(slot_grad, n, cap).astype(BF16)
    else:
        back_out[...] = slabs(slot_grad.astype(BF16), n, cap)
    every(lambda d: back_copy(d, me).start())
    back_in[pl.ds(me, 1)] = back_out[pl.ds(me, 1)]

    kgrad[...] = jnp.zeros((ext, cw), F32)
    vgrad[...] = jnp.zeros((ext, cw), F32)
    near_c = near_f * inv

    def near_back(h, _):
        here = col_head == h
        keys = kx[...].reshape(ext, cw)
        qh = jnp.where(here, q_ref[...], jnp.zeros((), BF16))
        dah = jnp.where(here, da_s[...], jnp.zeros((), BF16))
        c = jnp.sum(jnp.where(lane == h, near_c, 0.0), axis=1, keepdims=True)
        dl = jnp.sum(jnp.where(lane == h, delta, 0.0), axis=1, keepdims=True)
        prob = exps[h] * c
        ds = (prob * (dprobs[h] - dl)).astype(BF16)
        qgrad[...] += jnp.where(here, dot(ds, keys), 0.0)
        kgrad[...] += dot_tn(ds, qh)
        vgrad[...] += dot_tn(prob.astype(BF16), dah)
        return _

    lax.fori_loop(0, heads, near_back, 0)
    for s, lo in ((0, 0), (1, 2 * nodes)):
        rim_out[s, :, :cw] = (kgrad[lo : lo + nodes, :] * scale).astype(BF16)
        rim_out[s, :, cw:] = vgrad[lo : lo + nodes, :].astype(BF16)

    @pl.when(me > 0)
    def _():
        rim_back(True).start()

    @pl.when(me < n - 1)
    def _():
        rim_back(False).start()

    half = n // 2
    for mine in (True, False):
        block = dot_tn(g_ref[...] if mine else g_oth[...], att)
        first = (hd if mine else 1 - hd) * half
        if drows % 16:
            wide[0, :, :cw] = block
            for i in range(half):
                dw_out[pl.ds(first + i, 1)] = wide[0, i * drows : (i + 1) * drows, :cw].astype(BF16)[None]
        else:
            dw_out[pl.ds(first, half)] = slabs(block.astype(BF16), half, drows)
    every(lambda d: dw_copy(d, me).start())
    dw_in[pl.ds(me, 1)] = dw_out[pl.ds(me, 1)]

    qg_ref[...] = (qgrad[...] * scale).astype(BF16)
    send_w.wait_recv()
    send_att.wait_recv()
    lo_ref[...] = (dot(att, w_ref[:, my_cols]) + dot(att_oth[...], w_oth[...])).astype(BF16)

    @pl.when(me > 0)
    def _():
        rim_back(False).wait_recv()

    @pl.when(me < n - 1)
    def _():
        rim_back(True).wait_recv()

    every(lambda s: back_copy(s, s).wait_recv())
    own = dot(rows_t[...], flat_of(back_in[...]))
    rim = rim_in[0].astype(F32) + rim_in[1].astype(F32)
    own_k = kgrad[nodes : 2 * nodes, :] * scale
    kg_ref[...] = (own[:, :cw] + rim[:, :cw] + own_k).astype(BF16)
    vg_ref[...] = (own[:, cw:] + rim[:, cw:] + vgrad[nodes : 2 * nodes, :]).astype(BF16)
    every(lambda s: dw_copy(s, s).wait_recv())
    dw_ref[...] = jnp.sum(dw_in[...].astype(F32), axis=0)

    def left(d):
        far_copy(d, me).wait_send()
        back_copy(d, me).wait_send()
        dw_copy(d, me).wait_send()

    every(left)
    send_g.wait_send()
    send_w.wait_send()
    send_att.wait_send()

    @pl.when(me > 0)
    def _():
        for c in rim_copies(True):
            c.wait_send()
        rim_back(True).wait_send()

    @pl.when(me < n - 1)
    def _():
        for c in rim_copies(False):
            c.wait_send()
        rim_back(False).wait_send()


def shards(
    n, q, k, v, out_weight, out_grad, far_bias, tile_list, tile_count, send_rows, expander_slot
):
    nodes, cw = q.shape
    heads = far_bias.shape[0]
    cap = send_rows.shape[2]
    deg = expander_slot.shape[1]
    drows = 2 * cw // n
    ext = 3 * nodes
    slots = n * cap
    dma = pltpu.SemaphoreType.DMA
    vm = pl.BlockSpec(memory_space=pltpu.VMEM)
    sm = pl.BlockSpec(memory_space=pltpu.SMEM)
    node_out = jax.ShapeDtypeStruct((nodes, cw), BF16)
    return pl.pallas_call(
        functools.partial(body, n),
        out_shape=(node_out, node_out, node_out, node_out, jax.ShapeDtypeStruct((drows, cw), F32)),
        in_specs=[vm, vm, vm, vm, vm, sm, sm, sm, vm, vm],
        out_specs=(vm, vm, vm, vm, vm),
        scratch_shapes=[
            pltpu.VMEM((3, nodes, cw), BF16),
            pltpu.VMEM((3, nodes, cw), BF16),
            pltpu.VMEM((n, cap, 2 * cw), BF16),
            pltpu.VMEM((n, cap, 2 * cw), BF16),
            pltpu.VMEM((n, cap, 2 * cw), BF16),
            pltpu.VMEM((n, cap, 2 * cw), BF16),
            pltpu.VMEM((nodes, cw), BF16),
            pltpu.VMEM((cw, cw), BF16),
            pltpu.VMEM((nodes, cw), BF16),
            pltpu.VMEM((nodes, cw), BF16),
            pltpu.VMEM((2, nodes, 2 * cw), BF16),
            pltpu.VMEM((2, nodes, 2 * cw), BF16),
            pltpu.VMEM((n, drows, cw), BF16),
            pltpu.VMEM((n, drows, cw), BF16),
            pltpu.VMEM((heads, nodes, ext), F32),
            pltpu.VMEM((heads, nodes, ext), F32),
            pltpu.VMEM((nodes, ext), F32),
            pltpu.VMEM((nodes, cw), F32),
            pltpu.VMEM((nodes, 128), F32),
            pltpu.VMEM((nodes, 128), F32),
            pltpu.VMEM((ext, cw), F32),
            pltpu.VMEM((ext, cw), F32),
            pltpu.VMEM((nodes, cw), F32),
            pltpu.VMEM((slots, deg * nodes), BF16),
            pltpu.VMEM((nodes, slots), BF16),
            pltpu.VMEM((nodes, cw), BF16),
            pltpu.VMEM((deg, nodes, 2 * cw), F32),
            dma((n,)), dma((n,)), dma((4,)), dma((4,)), dma((n,)), dma((n,)),
            dma((2,)), dma((2,)), dma((n,)), dma((n,)), dma((3,)), dma((3,)),
        ],
        compiler_params=pltpu.CompilerParams(
            collective_id=0, has_side_effects=True, vmem_limit_bytes=48 * 1024 * 1024
        ),
        name="exphormer",
    )(
        q, k, v, out_weight, out_grad, far_bias, tile_list, tile_count,
        send_rows.reshape(1, slots), expander_slot,
    )


def solution(mesh):
    in_specs = (
        P("dom", "head"),
        P("dom", "head"),
        P("dom", "head"),
        P("head", None),
        P("dom", "head"),
        P("head"),
        P("dom", None),
        P("dom"),
        P("dom", None, None),
        P("dom", None),
    )
    out_specs = (P("dom", "head"),) * 5
    return jax.shard_map(
        functools.partial(shards, mesh.shape["dom"]),
        mesh=mesh, in_specs=in_specs, out_specs=out_specs, check_vma=False,
    )
```

time: 231 us -> 92.6 us (0.40)
  the two profiles are of different devices: /device:TPU:0 before, /device:TPU:25 now
where the time goes in v1:
time: 92.6 us; the launch traced here: 92.4 us
  Pallas kernels  83.3 us (90%)
  local copies, waits for them, and re-layouts  8.38 us (9%)
    pallas_call x1, Pallas kernels, shards(): pl.pallas_call(functools.partial(body, n), out_shape=(node_out, node_out,...  83.3 us
    unnamed x24, local copies, waits for them, and re-layouts  7.57 us

profile of v1, /device:TPU:25, one launch (start us, length us, event | category | flops | bytes accessed | tf_op | source)
XLA Modules:
  0.0 92.4 jit_solution(6904527040485899249)
XLA Ops:
  0.6 0.0 copy-start.8
  0.6 0.0 copy-start.1
  0.7 0.8 reshape.13.rows_ref
  1.5 0.0 copy-done.8
  1.5 0.0 copy-start.5
  1.5 0.0 copy-start.6
  1.5 0.0 copy-start.7
  1.5 0.1 copy.15.slot_ref
  1.6 0.0 copy-done.1
  1.6 0.5 copy-done.5
  2.2 0.0 copy-done.6
  2.2 0.0 copy-done.7
  2.2 0.0 copy-start
  2.2 0.9 %copy-done = bf16[256,512]{1,0:T(8,128)(2,1)S(1)} copy-done((bf16[256,512]{1,0:T(8,128)(2,1)S(1)}, bf16[256,512]{1,0:T(8,128)(2,1)}, u32[]{:S(2)}) %copy-start) | copy-done | bytes 262168
  3.1 0.0 copy-start.2
  3.1 0.9 copy-done.2
  4.0 0.0 copy-start.3
  4.0 0.9 copy-done.3
  4.9 0.0 copy-start.4
  4.9 0.9 copy-done.4
  5.8 83.3 %exphormer.1 = (bf16[256,256]{1,0:T(8,128)(2,1)S(1)}, bf16[256,256]{1,0:T(8,128)(2,1)S(1)}, bf16[256,256]{1,0:T(8,128)(2,1)S(1)}, bf16[256,256]{1,0:T(8,128)(2,1)S(1)}, f32[32,256]{1,0:T(8,128)S(1)}) custom-call(bf16[256,256]{1,0:T(8,128)(2,1)S(1)} %copy-done.1, bf16[256,256]{1,0:T(8,128)(2,1)S(1)} %copy-done.2, bf16[256,256]{1,0:T(8,128)(2,1)S(1)} %copy-done.3, ...), custom_call_target="tpu_custom_call" | custom-call | tf_op jit(solution)/shard_map/exphormer/pallas_call | solution.py:371
  89.1 0.7 copy.21
  89.8 0.7 copy.22
  90.4 0.7 copy.23
  91.1 0.7 copy.24
  91.8 0.6 copy.25
Async XLA Ops:
  0.6 0.8 copy-start.8
  0.6 1.0 %copy-start.1 = (bf16[256,256]{1,0:T(8,128)(2,1)S(1)}, bf16[256,256]{1,0:T(8,128)(2,1)}, u32[]{:S(2)}) copy-start(bf16[256,256]{1,0:T(8,128)(2,1)} %q_ref.1) | copy-start | bytes 393220
  1.5 0.7 copy-start.5
  1.5 0.7 copy-start.6
  1.5 0.7 copy-start.7
  2.2 0.9 %copy-start = (bf16[256,512]{1,0:T(8,128)(2,1)S(1)}, bf16[256,512]{1,0:T(8,128)(2,1)}, u32[]{:S(2)}) copy-start(bf16[256,512]{1,0:T(8,128)(2,1)} %w_ref.1) | copy-start | bytes 786436
  3.1 0.9 copy-start.2
  4.0 0.9 copy-start.3
  4.9 0.9 copy-start.4

commit v2 on v1

--- a/solution.py
+++ b/solution.py
@@ -1,4 +1,5 @@
 import functools
+import math
 
 import jax
 import jax.numpy as jnp
@@ -47,16 +48,17 @@
 
 
 def body(
-    n, q_ref, k_ref, v_ref, w_ref, g_ref, bias_ref, list_ref, count_ref, rows_ref, slot_ref,
+    n, q_hbm, k_hbm, v_hbm, w_hbm, g_hbm, bias_ref, list_ref, count_ref, send_ref, slot_ref,
     lo_ref, qg_ref, kg_ref, vg_ref, dw_ref,
-    kx, vx, out_far, in_far, back_out, back_in, g_oth, w_oth, att_mine, att_oth,
-    rim_out, rim_in, dw_out, dw_in, exps, dprobs, mask_s, near_mix, near_max, near_sum,
+    q_ref, w_ref, g_ref, rows_ref, hots, kx, vx, out_far, in_far, back_out, back_in, g_oth, w_oth, att_mine, att_oth,
+    rim_out, rim_in, dw_out, dw_in, dw2_out, dw2_in, exps, dprobs, far_grad, mask_s, near_mix, near_max, near_sum,
     kgrad, vgrad, qgrad, far_t, rows_t, da_s, wide,
-    far_ss, far_rs, rim_ss, rim_rs, bck_ss, bck_rs, rbk_ss, rbk_rs, dw_ss, dw_rs, hd_ss, hd_rs,
+    far_ss, far_rs, rim_ss, rim_rs, bck_ss, bck_rs, rbk_ss, rbk_rs, dw_ss, dw_rs, dw2_ss, dw2_rs, hd_ss, hd_rs,
+    in_sem,
 ):
     me = lax.axis_index("dom")
     hd = lax.axis_index("head")
-    nodes, cw = q_ref.shape
+    nodes, cw = q_hbm.shape
     heads = bias_ref.shape[0]
     hsize = cw // heads
     scale = hsize ** (-0.5)
@@ -65,7 +67,24 @@
     deg = slot_ref.shape[1]
     tpd = nodes // TILE
     drows = dw_ref.shape[0]
+    inner = dw_out.shape[0]
+    outer = n // inner
     prev, nxt = lax.rem(me + n - 1, n), lax.rem(me + 1, n)
+
+    loads = [
+        pltpu.make_async_copy(src, dst, in_sem.at[i])
+        for i, (src, dst) in enumerate(
+            (
+                (k_hbm, kx.at[1]),
+                (v_hbm, vx.at[1]),
+                (g_hbm, g_ref),
+                (w_hbm, w_ref),
+                (q_hbm, q_ref),
+            )
+        )
+    ]
+    for c in loads:
+        c.start()
 
     barrier = pltpu.get_barrier_semaphore()
 
@@ -98,8 +117,8 @@
         d, at = (prev, 2) if low else (nxt, 0)
         s = 0 if low else 2
         return (
-            to_dom(k_ref, kx.at[at], rim_ss.at[s], rim_rs.at[s], d),
-            to_dom(v_ref, vx.at[at], rim_ss.at[s + 1], rim_rs.at[s + 1], d),
+            to_dom(kx.at[1], kx.at[at], rim_ss.at[s], rim_rs.at[s], d),
+            to_dom(vx.at[1], vx.at[at], rim_ss.at[s + 1], rim_rs.at[s + 1], d),
         )
 
     def rim_back(low):
@@ -112,42 +131,64 @@
     def back_copy(d, s):
         return to_dom(back_out.at[d], back_in.at[s], bck_ss.at[d], bck_rs.at[s], d)
 
-    def dw_copy(d, s):
-        return to_dom(dw_out.at[d], dw_in.at[s], dw_ss.at[d], dw_rs.at[s], d)
-
-    def every(fn):
+    my_in, my_out = lax.rem(me, inner), me // inner
+
+    def dw_copy(j, s):
+        return to_dom(dw_out.at[j], dw_in.at[s], dw_ss.at[j], dw_rs.at[s], my_out * inner + j)
+
+    def dw2_copy(o, s):
+        return to_dom(dw2_out.at[o], dw2_in.at[s], dw2_ss.at[o], dw2_rs.at[s], o * inner + my_in)
+
+    def partner(a, i, size):
+        if size & (size - 1):
+            return lax.rem(a + i, size)
+        bit, out = 1, 0
+        while bit < size:
+            out = out + ((a // bit + i // bit) % 2) * bit
+            bit *= 2
+        return out
+
+    def every(fn, at=None, size=n):
+        at = me if at is None else at
+
         def step(i, _):
-            fn(lax.rem(me + i, n))
+            fn(partner(at, i, size))
             return _
 
-        lax.fori_loop(1, n, step, 0)
-
-    kv = jnp.concatenate([k_ref[...], v_ref[...]], axis=1)
-    row_col = jnp.transpose(jnp.broadcast_to(rows_ref[...], (128, slots)))[:, 0:1]
-    pick = (row_col == iota((slots, nodes), 1)).astype(F32).astype(BF16)
-    picked = dot(pick, kv)
+        lax.fori_loop(1, size, step, 0)
+
+    rows_ref[...] = jnp.zeros(rows_ref.shape, jnp.int32)
+    rows_ref[:n, :cap] = send_ref[0]
+    for c in loads[:2]:
+        c.wait()
+
+    @pl.when(me > 0)
+    def _():
+        for c in rim_copies(True):
+            c.start()
+
+    @pl.when(me < n - 1)
+    def _():
+        for c in rim_copies(False):
+            c.start()
+
+    loads[2].wait()
+    send_g.start()
+    kv = jnp.concatenate([kx[1], vx[1]], axis=1)
+    row_cols = jnp.transpose(rows_ref[...])
+    row_col = jnp.concatenate([row_cols[:cap, d : d + 1] for d in range(n)], axis=0)
+    pick = (row_col == iota((slots, nodes), 1)).astype(F32)
+    picked = dot(pick.astype(BF16), kv)
     if cap % 16:
         out_far[...] = slabs(picked, n, cap).astype(BF16)
     else:
         out_far[...] = slabs(picked.astype(BF16), n, cap)
     every(lambda d: far_copy(d, me).start())
-    send_g.start()
-
-    @pl.when(me > 0)
-    def _():
-        for c in rim_copies(True):
-            c.start()
-
-    @pl.when(me < n - 1)
-    def _():
-        for c in rim_copies(False):
-            c.start()
-
+
+    loads[3].wait()
     send_w.start()
+    loads[4].wait()
     in_far[pl.ds(me, 1)] = out_far[pl.ds(me, 1)]
-
-    kx[1] = k_ref[...]
-    vx[1] = v_ref[...]
 
     @pl.when(me == 0)
     def _():
@@ -161,9 +202,10 @@
         vx[2] = jnp.zeros((nodes, cw), BF16)
         rim_in[1] = jnp.zeros(rim_in.shape[1:], BF16)
 
-    rows_t[...] = (rows_ref[...] == iota((nodes, slots), 0)).astype(F32).astype(BF16)
+    rows_t[...] = jnp.transpose(pick).astype(BF16)
     for e in range(deg):
         col = slot_ref[:, e : e + 1]
+        hots[e] = (col == iota((nodes, slots), 1)).astype(F32).astype(BF16)
         row = jnp.transpose(jnp.broadcast_to(col, (nodes, 128)))[0:1, :]
         far_t[:, e * nodes : (e + 1) * nodes] = (row == iota((slots, nodes), 0)).astype(F32).astype(BF16)
     for t in range(tpd):
@@ -213,19 +255,18 @@
 
     lax.fori_loop(0, heads, near_head, 0)
 
-    every(lambda s: far_copy(s, s).wait_recv())
     fold = (iota((cw, 128), 0) // hsize == iota((cw, 128), 1)).astype(F32).astype(BF16)
     spread = (iota((128, cw), 0) == iota((128, cw), 1) // hsize).astype(F32).astype(BF16)
     bias = jnp.zeros((1, 128), F32)
     for h in range(heads):
         bias = jnp.where(iota((1, 128), 1) == h, bias_ref[h], bias)
-    received = flat_of(in_far[...])
     q32 = q_ref[...].astype(F32)
     da32 = da_s[...].astype(F32)
+    every(lambda s: far_copy(s, s).wait_recv())
+    received = flat_of(in_far[...])
     far_s = []
     for e in range(deg):
-        hot = (slot_ref[:, e : e + 1] == iota((nodes, slots), 1)).astype(F32).astype(BF16)
-        wide[e] = dot(hot, received)
+        wide[e] = dot(hots[e], received)
         far_s.append(split_dot(q32 * wide[e, :, :cw], fold) * scale + bias)
     top_n = near_max[...]
     top = top_n
@@ -257,12 +298,27 @@
             )
         )
     qgrad[...] = qg
-    slot_grad = dot(far_t[...], jnp.concatenate(parts, axis=0))
-    if cap % 16:
-        back_out[...] = slabs(slot_grad, n, cap).astype(BF16)
-    else:
-        back_out[...] = slabs(slot_grad.astype(BF16), n, cap)
-    every(lambda d: back_copy(d, me).start())
+    far_grad[...] = jnp.concatenate(parts, axis=0)
+    group = inner * cap
+
+    def send_back(i, _):
+        o = partner(my_out, outer - 1 - i, outer)
+        slot_grad = dot(far_t[pl.ds(pl.multiple_of(o * group, group), group), :], far_grad[...])
+        if cap % 16:
+            block = slabs(slot_grad, inner, cap).astype(BF16)
+        else:
+            block = slabs(slot_grad.astype(BF16), inner, cap)
+        back_out[pl.ds(o * inner, inner)] = block
+        for j in range(inner):
+            d = o * inner + partner(my_in, j, inner)
+
+            @pl.when(d != me)
+            def go():
+                back_copy(d, me).start()
+
+        return _
+
+    lax.fori_loop(0, outer, send_back, 0)
     back_in[pl.ds(me, 1)] = back_out[pl.ds(me, 1)]
 
     kgrad[...] = jnp.zeros((ext, cw), F32)
@@ -296,24 +352,33 @@
     def _():
         rim_back(False).start()
 
-    half = n // 2
+    half = outer // 2
     for mine in (True, False):
         block = dot_tn(g_ref[...] if mine else g_oth[...], att)
         first = (hd if mine else 1 - hd) * half
         if drows % 16:
             wide[0, :, :cw] = block
-            for i in range(half):
-                dw_out[pl.ds(first + i, 1)] = wide[0, i * drows : (i + 1) * drows, :cw].astype(BF16)[None]
+            for i in range(half * inner):
+                dw_out[i % inner, pl.ds(first + i // inner, 1)] = (
+                    wide[0, i * drows : (i + 1) * drows, :cw].astype(BF16)[None]
+                )
         else:
-            dw_out[pl.ds(first, half)] = slabs(block.astype(BF16), half, drows)
-    every(lambda d: dw_copy(d, me).start())
-    dw_in[pl.ds(me, 1)] = dw_out[pl.ds(me, 1)]
+            cut = block.astype(BF16).reshape(half, inner, drows, cw)
+            for j in range(inner):
+                dw_out[j, pl.ds(first, half)] = cut[:, j]
+    every(lambda j: dw_copy(j, my_in).start(), my_in, inner)
+    dw_in[pl.ds(my_in, 1)] = dw_out[pl.ds(my_in, 1)]
 
     qg_ref[...] = (qgrad[...] * scale).astype(BF16)
     send_w.wait_recv()
     send_att.wait_recv()
     lo_ref[...] = (dot(att, w_ref[:, my_cols]) + dot(att_oth[...], w_oth[...])).astype(BF16)
 
+    every(lambda s: dw_copy(s, s).wait_recv(), my_in, inner)
+    dw2_out[...] = jnp.sum(dw_in[...].astype(F32), axis=0).astype(BF16)
+    every(lambda o: dw2_copy(o, my_out).start(), my_out, outer)
+    dw2_in[pl.ds(my_out, 1)] = dw2_out[pl.ds(my_out, 1)]
+
     @pl.when(me > 0)
     def _():
         rim_back(False).wait_recv()
@@ -322,21 +387,22 @@
     def _():
         rim_back(True).wait_recv()
 
+    every(lambda s: dw2_copy(s, s).wait_recv(), my_out, outer)
+    dw_ref[...] = jnp.sum(dw2_in[...].astype(F32), axis=0)
     every(lambda s: back_copy(s, s).wait_recv())
     own = dot(rows_t[...], flat_of(back_in[...]))
     rim = rim_in[0].astype(F32) + rim_in[1].astype(F32)
     own_k = kgrad[nodes : 2 * nodes, :] * scale
     kg_ref[...] = (own[:, :cw] + rim[:, :cw] + own_k).astype(BF16)
     vg_ref[...] = (own[:, cw:] + rim[:, cw:] + vgrad[nodes : 2 * nodes, :]).astype(BF16)
-    every(lambda s: dw_copy(s, s).wait_recv())
-    dw_ref[...] = jnp.sum(dw_in[...].astype(F32), axis=0)
 
     def left(d):
         far_copy(d, me).wait_send()
         back_copy(d, me).wait_send()
-        dw_copy(d, me).wait_send()
 
     every(left)
+    every(lambda j: dw_copy(j, my_in).wait_send(), my_in, inner)
+    every(lambda o: dw2_copy(o, my_out).wait_send(), my_out, outer)
     send_g.wait_send()
     send_w.wait_send()
     send_att.wait_send()
@@ -352,6 +418,11 @@
         for c in rim_copies(False):
             c.wait_send()
         rim_back(False).wait_send()
+
+
+def place(*refs):
+    for i in range(5):
+        refs[5 + i][...] = refs[i][...]
 
 
 def shards(
@@ -362,18 +433,25 @@
     cap = send_rows.shape[2]
     deg = expander_slot.shape[1]
     drows = 2 * cw // n
+    inner = math.gcd(n, 4)
     ext = 3 * nodes
     slots = n * cap
     dma = pltpu.SemaphoreType.DMA
     vm = pl.BlockSpec(memory_space=pltpu.VMEM)
     sm = pl.BlockSpec(memory_space=pltpu.SMEM)
     node_out = jax.ShapeDtypeStruct((nodes, cw), BF16)
-    return pl.pallas_call(
+    anywhere = pl.BlockSpec(memory_space=pl.ANY)
+    outs = pl.pallas_call(
         functools.partial(body, n),
         out_shape=(node_out, node_out, node_out, node_out, jax.ShapeDtypeStruct((drows, cw), F32)),
-        in_specs=[vm, vm, vm, vm, vm, sm, sm, sm, vm, vm],
+        in_specs=[anywhere] * 5 + [sm] * 3 + [vm] * 2,
         out_specs=(vm, vm, vm, vm, vm),
         scratch_shapes=[
+            pltpu.VMEM((nodes, cw), BF16),
+            pltpu.VMEM((cw, 2 * cw), BF16),
+            pltpu.VMEM((nodes, cw), BF16),
+            pltpu.VMEM((128, 128), jnp.int32),
+            pltpu.VMEM((deg, nodes, slots), BF16),
             pltpu.VMEM((3, nodes, cw), BF16),
             pltpu.VMEM((3, nodes, cw), BF16),
             pltpu.VMEM((n, cap, 2 * cw), BF16),
@@ -386,10 +464,13 @@
             pltpu.VMEM((nodes, cw), BF16),
             pltpu.VMEM((2, nodes, 2 * cw), BF16),
             pltpu.VMEM((2, nodes, 2 * cw), BF16),
-            pltpu.VMEM((n, drows, cw), BF16),
-            pltpu.VMEM((n, drows, cw), BF16),
+            pltpu.VMEM((inner, n // inner, drows, cw), BF16),
+            pltpu.VMEM((inner, n // inner, drows, cw), BF16),
+            pltpu.VMEM((n // inner, drows, cw), BF16),
+            pltpu.VMEM((n // inner, drows, cw), BF16),
             pltpu.VMEM((heads, nodes, ext), F32),
             pltpu.VMEM((heads, nodes, ext), F32),
+            pltpu.VMEM((deg * nodes, 2 * cw), BF16),
             pltpu.VMEM((nodes, ext), F32),
             pltpu.VMEM((nodes, cw), F32),
             pltpu.VMEM((nodes, 128), F32),
@@ -402,16 +483,24 @@
             pltpu.VMEM((nodes, cw), BF16),
             pltpu.VMEM((deg, nodes, 2 * cw), F32),
             dma((n,)), dma((n,)), dma((4,)), dma((4,)), dma((n,)), dma((n,)),
-            dma((2,)), dma((2,)), dma((n,)), dma((n,)), dma((3,)), dma((3,)),
+            dma((2,)), dma((2,)), dma((inner,)), dma((inner,)), dma((n // inner,)), dma((n // inner,)),
+            dma((3,)), dma((3,)), dma((5,)),
         ],
         compiler_params=pltpu.CompilerParams(
-            collective_id=0, has_side_effects=True, vmem_limit_bytes=48 * 1024 * 1024
+            collective_id=0, has_side_effects=True, vmem_limit_bytes=60 * 1024 * 1024
         ),
         name="exphormer",
     )(
         q, k, v, out_weight, out_grad, far_bias, tile_list, tile_count,
-        send_rows.reshape(1, slots), expander_slot,
+        send_rows, expander_slot,
     )
+    return pl.pallas_call(
+        place,
+        out_shape=tuple(jax.ShapeDtypeStruct(o.shape, o.dtype) for o in outs),
+        in_specs=[vm] * 5,
+        out_specs=(vm,) * 5,
+        name="place",
+    )(*outs)
 
 
 def solution(mesh):

time: 92.6 us -> 77.4 us (0.84)
  the two profiles are of different devices: /device:TPU:25 before, /device:TPU:0 now
where the time goes in v2:
time: 77.4 us; the launch traced here: 77.2 us
  Pallas kernels  75.1 us (97%)
  local copies, waits for them, and re-layouts  1.48 us (2%)
    pallas_call x1, Pallas kernels, shards(): pl.pallas_call(functools.partial(body, n), out_shape=(node_out, node_out,...  73.2 us
    pallas_call x1, Pallas kernels, shards(): pl.pallas_call(place, out_shape=tuple((jax.ShapeDtypeStruct(o.shape, o.dt...  1.9 us

profile of v2, /device:TPU:0, one launch (start us, length us, event | category | flops | bytes accessed | tf_op | source)
XLA Modules:
  0.0 77.2 jit_solution(8791887885593595271)
XLA Ops:
  0.6 1.5 %copy.15.slot_ref = s32[256,3]{1,0:T(8,128)} copy(s32[256,3]{0,1:T(4,128)} %param.19) | data formatting | bytes 6144 | tf_op args[9]
  2.1 73.2 %exphormer.1 = (bf16[256,256]{1,0:T(8,128)(2,1)}, bf16[256,256]{1,0:T(8,128)(2,1)}, bf16[256,256]{1,0:T(8,128)(2,1)}, bf16[256,256]{1,0:T(8,128)(2,1)}, f32[32,256]{1,0:T(8,128)}) custom-call(bf16[256,256]{1,0:T(8,128)(2,1)} %q_hbm.1, bf16[256,256]{1,0:T(8,128)(2,1)} %k_hbm.1, bf16[256,256]{1,0:T(8,128)(2,1)} %v_hbm.1, bf16[256,512]{1,0:T(8,128)(2,1)} %w_hbm.1, ...), custom_call_target="tpu_custom_call" | custom-call | tf_op jit(solution)/shard_map/exphormer/pallas_call | solution.py:444
  75.4 1.9 %place.1 = (bf16[256,256]{1,0:T(8,128)(2,1)}, bf16[256,256]{1,0:T(8,128)(2,1)}, bf16[256,256]{1,0:T(8,128)(2,1)}, bf16[256,256]{1,0:T(8,128)(2,1)}, f32[32,256]{1,0:T(8,128)}) custom-call(bf16[256,256]{1,0:T(8,128)(2,1)} %get-tuple-element.10.refs_0_, bf16[256,256]{1,0:T(8,128)(2,1)} %get-tuple-element.11.refs_1_, ...), custom_call_target="tpu_custom_call" | custom-call | tf_op jit(solution)/shard_map/place/pallas_call | solution.py:497

commit v3 on v2

--- a/solution.py
+++ b/solution.py
@@ -64,7 +64,7 @@
     scale = hsize ** (-0.5)
     cap = out_far.shape[1]
     slots = n * cap
-    deg = slot_ref.shape[1]
+    deg = slot_ref.shape[0]
     tpd = nodes // TILE
     drows = dw_ref.shape[0]
     inner = dw_out.shape[0]
@@ -204,9 +204,9 @@
 
     rows_t[...] = jnp.transpose(pick).astype(BF16)
     for e in range(deg):
-        col = slot_ref[:, e : e + 1]
+        row = slot_ref[e : e + 1, :]
+        col = jnp.transpose(jnp.broadcast_to(row, (128, nodes)))[:, 0:1]
         hots[e] = (col == iota((nodes, slots), 1)).astype(F32).astype(BF16)
-        row = jnp.transpose(jnp.broadcast_to(col, (nodes, 128)))[0:1, :]
         far_t[:, e * nodes : (e + 1) * nodes] = (row == iota((slots, nodes), 0)).astype(F32).astype(BF16)
     for t in range(tpd):
         for c in range(3 * tpd):
@@ -492,7 +492,7 @@
         name="exphormer",
     )(
         q, k, v, out_weight, out_grad, far_bias, tile_list, tile_count,
-        send_rows, expander_slot,
+        send_rows, expander_slot.T,
     )
     return pl.pallas_call(
         place,

time: 77.4 us -> 75.8 us (0.979)
  local copies, waits for them, and re-layouts: 1.48 us -> 0 us
    unnamed x1 -> x0, local copies, waits for them, and re-layouts: 1.48 us -> none
where the time goes in v3:
time: 75.8 us; the launch traced here: 75.6 us
  Pallas kernels  74.9 us (99%)
    pallas_call x1, Pallas kernels, shards(): pl.pallas_call(functools.partial(body, n), out_shape=(node_out, node_out,...  73 us
    pallas_call x1, Pallas kernels, shards(): pl.pallas_call(place, out_shape=tuple((jax.ShapeDtypeStruct(o.shape, o.dt...  1.9 us

profile of v3, /device:TPU:0, one launch (start us, length us, event | category | flops | bytes accessed | tf_op | source)
XLA Modules:
  0.0 75.6 jit_solution(15743446126005615772)
XLA Ops:
  0.6 73.0 %exphormer.1 = (bf16[256,256]{1,0:T(8,128)(2,1)}, bf16[256,256]{1,0:T(8,128)(2,1)}, bf16[256,256]{1,0:T(8,128)(2,1)}, bf16[256,256]{1,0:T(8,128)(2,1)}, f32[32,256]{1,0:T(8,128)}) custom-call(bf16[256,256]{1,0:T(8,128)(2,1)} %q_hbm.1, bf16[256,256]{1,0:T(8,128)(2,1)} %k_hbm.1, bf16[256,256]{1,0:T(8,128)(2,1)} %v_hbm.1, bf16[256,512]{1,0:T(8,128)(2,1)} %w_hbm.1, ...), custom_call_target="tpu_custom_call" | custom-call | tf_op jit(solution)/shard_map/exphormer/pallas_call | solution.py:444
  73.7 1.9 %place.1 = (bf16[256,256]{1,0:T(8,128)(2,1)}, bf16[256,256]{1,0:T(8,128)(2,1)}, bf16[256,256]{1,0:T(8,128)(2,1)}, bf16[256,256]{1,0:T(8,128)(2,1)}, f32[32,256]{1,0:T(8,128)}) custom-call(bf16[256,256]{1,0:T(8,128)(2,1)} %get-tuple-element.10.refs_0_, bf16[256,256]{1,0:T(8,128)(2,1)} %get-tuple-element.11.refs_1_, ...), custom_call_target="tpu_custom_call" | custom-call | tf_op jit(solution)/shard_map/place/pallas_call | solution.py:497
